TPU v7x, 32 devices: a whole 2x2x4 slice. The times are simulated.
32 devices in a mesh: case: 2 (over y), wall: 4 (over z), azim: 4 (over x, core).
Axes of the slice: x: 2, y: 2, z: 4, core: 2. Of those that a mesh axis runs over, the one named last changes fastest.
Arguments:
- state: float32 [12, 2, 32, 512], P(None, 'case', 'wall', 'azim'), parts along dimension 1, may hold values from 0.5 to 1.5
- courant: float32 [2, 32, 512], P('case', 'wall', 'azim'), parts along dimension 0, may hold values from -0.6 to 0.6
- cross_sections: float32 [64], replicated, may hold values from 0.02 to 0.6
- band_fractions: float32 [64], replicated, may hold values from 0.02 to 0.2
- absorb_index: int32 [11, 16], replicated, may hold values from 0 to 63
- band_index: int32 [16], replicated, may hold values from 0 to 63
Outputs:
- new_state: float32 [12, 2, 32, 512], P(None, 'case', 'wall', 'azim'), parts along dimension 1
- wall_flux: float32 [2, 512], P('case', 'azim'), parts along dimension 0
There are 2 independent parts, one for each index of `case`. A program takes and returns all parts, laid end to end along the dimension named above; an argument that names none is the same for every part. Nothing has to cross between parts.
All inputs are finite; a program needn't handle non-finite values.
Results may differ from a plain program's by a relative error of at most 0.0003.
Values sent between devices are 32-bit elements; how exact they have to be, the bound alone decides.
A program may use at most 64 MiB of HBM per device.

v0:
```python
import jax
import jax.numpy as jnp
from jax import lax
from jax.sharding import PartitionSpec as P

KERNEL_WEIGHTS = (0.55, 0.45)
KERNEL_RATES = (1.15, 3.4)
FILTER_STRENGTH = 0.02
COUPLING = 0.1


def with_halo(block, sides, width):
    for axis, dim in sides:
        count = lax.axis_size(axis)
        forward = [(i, i + 1) for i in range(count - 1)]
        forward.append((count - 1, 0))
        backward = [(target, source) for source, target in forward]
        low = lax.ppermute(
            lax.slice_in_dim(block, block.shape[dim] - width, None, axis=dim), axis, forward
        )
        high = lax.ppermute(lax.slice_in_dim(block, 0, width, axis=dim), axis, backward)
        block = jnp.concatenate([low, block, high], axis=dim)
    return block


def band_tables(absorb_index, band_index, cross_sections, band_fractions):
    entries = cross_sections.shape[0]
    table_slots = lax.broadcasted_iota(jnp.int32, (1, 1, entries), 2)
    spectral_absorber_area = jnp.sum(
        jnp.where(absorb_index[:, :, None] == table_slots, cross_sections[None, None, :], 0.0),
        axis=2,
    )
    chosen_values = jnp.where(band_index[:, None] == table_slots[0], band_fractions[None, :], 0.0)
    return (spectral_absorber_area, jnp.sum(chosen_values, axis=1))


def viewing_line_irradiance(
    kinetic_heat_level,
    species_concentrations,
    spectral_absorber_area,
    spectral_fraction_weight,
    mesh_cell_width,
    viewing_line_dimension,
):
    absorption = jnp.einsum(
        "kb,kij->bij",
        spectral_absorber_area,
        species_concentrations,
        precision=lax.Precision.HIGHEST,
    )
    optical_thickness_step = absorption * mesh_cell_width
    optical_depth = (
        lax.cumsum(optical_thickness_step, viewing_line_dimension) - 0.5 * optical_thickness_step
    )
    radiated_energy_rate = (
        spectral_fraction_weight[:, None, None]
        * kinetic_heat_level[None] ** 4
        * optical_thickness_step
    )
    net_flux = 0.0
    wall_flux = 0.0
    for weight, decay_rate in zip(KERNEL_WEIGHTS, KERNEL_RATES):
        growth = jnp.exp(decay_rate * optical_depth)
        falloff = jnp.exp(-decay_rate * optical_depth)
        upward = falloff * lax.cumsum(radiated_energy_rate * growth, viewing_line_dimension)
        tail_sum = lax.cumsum(radiated_energy_rate * falloff, viewing_line_dimension, reverse=True)
        net_flux = net_flux + weight * jnp.sum(upward - growth * tail_sum, axis=0)
        wall_flux = wall_flux + weight * jnp.sum(
            lax.index_in_dim(tail_sum, 0, viewing_line_dimension, keepdims=False), axis=0
        )
    return (net_flux, wall_flux)


def edge_pad(net_flux, viewing_line_dimension):
    count = net_flux.shape[viewing_line_dimension]
    first_row = lax.slice_in_dim(net_flux, 0, 1, axis=viewing_line_dimension)
    last_row = lax.slice_in_dim(net_flux, count - 1, count, axis=viewing_line_dimension)
    return jnp.concatenate([first_row, net_flux, last_row], viewing_line_dimension)


def divergence(padded, viewing_line_dimension, mesh_cell_width):
    count = padded.shape[viewing_line_dimension] - 2
    before = lax.slice_in_dim(padded, 0, count, axis=viewing_line_dimension)
    after = lax.slice_in_dim(padded, 2, count + 2, axis=viewing_line_dimension)
    return (before - after) / (2.0 * mesh_cell_width)


def tendency(shifted, courant, heating):
    gradient = (
        45.0 * (shifted(1) - shifted(-1))
        - 9.0 * (shifted(2) - shifted(-2))
        + (shifted(3) - shifted(-3))
    ) / 60.0
    smoothing = (
        shifted(-3)
        + shifted(3)
        - 6.0 * (shifted(-2) + shifted(2))
        + 15.0 * (shifted(-1) + shifted(1))
        - 20.0 * shifted(0)
    )
    change_sum = FILTER_STRENGTH * smoothing - courant[None] * gradient
    return change_sum.at[0].add(COUPLING * heating)


def radiate(current, spectral_absorber_area, spectral_fraction_weight, mesh_cell_width):
    components, stations, row_count, col_count = current.shape
    line_data = jnp.transpose(current, (0, 2, 1, 3)).reshape(
        components, row_count, stations * col_count
    )
    gathered = lax.all_gather(line_data, "wall", axis=1, tiled=True)
    net_flux, wall_flux = viewing_line_irradiance(
        gathered[0],
        gathered[1:],
        spectral_absorber_area,
        spectral_fraction_weight,
        mesh_cell_width,
        1,
    )
    padded = edge_pad(net_flux, 0)
    row_start = lax.axis_index("wall") * row_count
    heating = divergence(
        lax.dynamic_slice_in_dim(padded, row_start, row_count + 2, 0), 0, mesh_cell_width
    )
    heating = jnp.transpose(heating.reshape(row_count, stations, col_count), (1, 0, 2))
    return (heating, wall_flux.reshape(stations, col_count))


def local(state, courant, cross_sections, band_fractions, absorb_index, band_index):
    spectral_absorber_area, spectral_fraction_weight = band_tables(
        absorb_index, band_index, cross_sections, band_fractions
    )
    mesh_cell_width = 1.0 / (state.shape[2] * lax.axis_size("wall"))
    col_count = state.shape[3]

    def segment_change(current):
        heating, wall_flux = radiate(
            current, spectral_absorber_area, spectral_fraction_weight, mesh_cell_width
        )
        padded = with_halo(current, (("azim", 3),), 3)

        def shifted(offset):
            return lax.slice_in_dim(padded, 3 + offset, 3 + offset + col_count, axis=3)

        return (tendency(shifted, courant, heating), wall_flux)

    first_change, first_flux = segment_change(state)
    middle = state + first_change
    second_change, second_flux = segment_change(middle)
    new_state = 0.5 * (state + middle + second_change)
    return (new_state, 0.5 * (first_flux + second_flux))


def solution(mesh):
    return jax.shard_map(
        local,
        mesh=mesh,
        in_specs=(P(None, "case", "wall", "azim"), P("case", "wall", "azim"), P(), P(), P(), P()),
        out_specs=(P(None, "case", "wall", "azim"), P("case", "azim")),
        check_vma=False,
    )
```

profile of v0, /device:TPU:0, one launch (start us, length us, event | category | flops | bytes accessed | tf_op | source)
XLA Modules:
  0.0 42.3 jit_solution(989441874617617582)
XLA Ops:
  0.6 0.0 copy-start
  0.6 1.0 %fusion.71 = (f32[12,1,8,3]{3,2,1,0:T(8,128)S(1)}, f32[12,1,8,3]{3,2,1,0:T(8,128)S(1)}) fusion(f32[12,1,8,128]{3,2,1,0:T(8,128)} %param.10), kind=kLoop, calls=%fused_computation.127 | loop fusion | bytes 4608 | tf_op jit(solution)/shard_map/slice | solution.py:21
  1.6 2.4 %collective-permute-start.1 = (f32[12,1,8,3]{3,2,1,0:T(8,128)S(1)}, f32[12,1,8,3]{3,2,1,0:T(8,128)S(1)}, u32[]{:S(2)}, u32[]{:S(2)}) collective-permute-start(f32[12,1,8,3]{3,2,1,0:T(8,128)S(1)} %get-tuple-element.34), channel_id=1, source_target_pairs={{1,0},{2,1},{3,2},{0,3},{5,4},{6,5},{7,6},{4,7},{9,8},{10,9},{11,1... | collective-permute-start | bytes 3464 | tf_op jit(solution)/shard_map/ppermute | solution.py:21
  4.0 0.0 collective-permute-start
  4.0 0.0 copy-done
  4.0 0.1 copy.53
  4.1 14.1 %all-gather = f32[12,1,32,128]{3,1,0,2:T(1,128)S(1)} all-gather(f32[12,1,8,128]{3,1,0,2:T(1,128)S(1)} %copy.53), channel_id=2, replica_groups=mesh['case'=2,'wall'=4,'azim'=4] {'wall'}, dimensions={2}, use_global_device_ids=true | all-gather | bytes 245760 | tf_op jit(solution)/shard_map/all_gather | solution.py:110
  18.2 0.0 copy-start.1
  18.2 0.0 copy-start.3
  18.3 0.6 %copy-done.1 = s32[11,16]{1,0:T(8,128)S(1)} copy-done((s32[11,16]{1,0:T(8,128)S(1)}, s32[11,16]{1,0:T(8,128)}, u32[]{:S(2)}) %copy-start.1) | copy-done | bytes 728
  18.9 0.0 copy-done.3
  18.9 0.2 select_reduce_fusion
  19.1 0.4 fusion.5
  19.5 0.0 copy-start.4
  19.6 0.0 copy-start.5
  19.6 0.6 %copy-done.4 = f32[64]{0:T(128)S(1)} copy-done((f32[64]{0:T(128)S(1)}, f32[64]{0:T(128)}, u32[]{:S(2)}) %copy-start.4) | copy-done | bytes 280
  20.2 0.0 copy-done.5
  20.2 0.2 select_reduce_fusion.1
  20.4 0.2 fusion.16
  20.7 0.2 fusion.21
  20.9 0.2 fusion.74
  21.1 0.2 fusion.75
  21.4 0.0 copy-start.2
  21.4 0.7 %copy-done.2 = f32[1,8,128]{2,1,0:T(8,128)S(1)} copy-done((f32[1,8,128]{2,1,0:T(8,128)S(1)}, f32[1,8,128]{2,1,0:T(8,128)}, u32[]{:S(2)}) %copy-start.2) | copy-done | bytes 4120
  22.1 0.0 collective-permute-done.1
  22.2 0.0 collective-permute-done
  22.2 0.2 multiply_subtract_fusion.1
  22.4 0.1 copy.56
  22.5 0.1 fusion.70
  22.5 13.8 %all-gather.1 = f32[12,1,32,128]{3,1,0,2:T(1,128)S(1)} all-gather(f32[12,1,8,128]{3,1,0,2:T(1,128)S(1)} %copy.56), channel_id=3, replica_groups=mesh['case'=2,'wall'=4,'azim'=4] {'wall'}, dimensions={2}, use_global_device_ids=true | all-gather | bytes 245760 | tf_op jit(solution)/shard_map/all_gather | solution.py:110
  36.4 0.4 fusion.4
  36.8 0.2 fusion.6
  37.1 0.2 fusion.11
  37.3 0.2 fusion.76
  37.6 0.2 fusion.77
  37.8 0.1 collective-permute-start.3
  37.9 0.5 %collective-permute-start.2 = (f32[12,1,8,3]{3,2,1,0:T(8,128)S(1)}, f32[12,1,8,3]{3,2,1,0:T(8,128)S(1)}, u32[]{:S(2)}, u32[]{:S(2)}) collective-permute-start(f32[12,1,8,3]{3,2,1,0:T(8,128)S(1)} %get-tuple-element.33), channel_id=1, source_target_pairs={{0,1},{1,2},{2,3},{3,0},{4,5},{5,6},{6,7},{7,4},{8,9},{9,10},{10,1... | collective-permute-start | bytes 3464 | tf_op jit(solution)/shard_map/ppermute | solution.py:18
  38.4 0.5 %multiply_bitcast_fusion.1 = f32[1,128]{1,0:T(1,128)} fusion(f32[128]{0:T(128)S(1)} %get-tuple-element.40, f32[128]{0:T(128)S(1)} %get-tuple-element.41, f32[128]{0:T(128)S(1)} %get-tuple-element.42, f32[128]{0:T(128)S(1)} %get-tuple-element.43), kind=kLoop, calls=%fused_computation.115 | loop fusion | flops 1024 | bytes 2560 | tf_op jit(solution)/shard_map/mul | solution.py:150
  38.9 0.7 %collective-permute-done.3 = f32[12,1,8,3]{3,2,1,0:T(8,128)S(1)} collective-permute-done((f32[12,1,8,3]{3,2,1,0:T(8,128)S(1)}, f32[12,1,8,3]{3,2,1,0:T(8,128)S(1)}, u32[]{:S(2)}, u32[]{:S(2)}) %collective-permute-start.3) | collective-permute-done | bytes 1184 | tf_op jit(solution)/shard_map/ppermute | solution.py:21
  39.7 1.8 %collective-permute-done.2 = f32[12,1,8,3]{3,2,1,0:T(8,128)S(1)} collective-permute-done((f32[12,1,8,3]{3,2,1,0:T(8,128)S(1)}, f32[12,1,8,3]{3,2,1,0:T(8,128)S(1)}, u32[]{:S(2)}, u32[]{:S(2)}) %collective-permute-start.2) | collective-permute-done | bytes 1184 | tf_op jit(solution)/shard_map/ppermute | solution.py:18
  41.5 0.2 multiply_subtract_fusion
  41.7 0.6 %add_multiply_fusion = f32[12,1,8,128]{3,2,1,0:T(8,128)} fusion(f32[12,1,8,128]{3,2,1,0:T(8,128)S(1)} %fusion.55, f32[12,1,8,128]{3,2,1,0:T(8,128)S(1)} %copy-done, f32[12,1,8,128]{3,2,1,0:T(8,128)S(1)} %add.105), kind=kLoop, calls=%fused_computation.75 | loop fusion | flops 36864 | bytes 196608 | tf_op jit(solution)/shard_map/mul | solution.py:149
  (20 shorter events, 0.3 us)
Async XLA Ops:
  0.6 3.4 %copy-start = (f32[12,1,8,128]{3,2,1,0:T(8,128)S(1)}, f32[12,1,8,128]{3,2,1,0:T(8,128)}, u32[]{:S(2)}) copy-start(f32[12,1,8,128]{3,2,1,0:T(8,128)} %param.10) | copy-start | bytes 147460
  1.6 20.5 %collective-permute-start.1 = (f32[12,1,8,3]{3,2,1,0:T(8,128)S(1)}, f32[12,1,8,3]{3,2,1,0:T(8,128)S(1)}, u32[]{:S(2)}, u32[]{:S(2)}) collective-permute-start(f32[12,1,8,3]{3,2,1,0:T(8,128)S(1)} %get-tuple-element.34), channel_id=1, source_target_pairs={{1,0},{2,1},{3,2},{0,3},{5,4},{6,5},{7,6},{4,7},{9,8},{10,9},{11,1... | collective-permute-start | bytes 3464 | tf_op jit(solution)/shard_map/ppermute | solution.py:21
  4.0 18.2 %collective-permute-start = (f32[12,1,8,3]{3,2,1,0:T(8,128)S(1)}, f32[12,1,8,3]{3,2,1,0:T(8,128)S(1)}, u32[]{:S(2)}, u32[]{:S(2)}) collective-permute-start(f32[12,1,8,3]{3,2,1,0:T(8,128)S(1)} %get-tuple-element.35), channel_id=1, source_target_pairs={{0,1},{1,2},{2,3},{3,0},{4,5},{5,6},{6,7},{7,4},{8,9},{9,10},{10,1... | collective-permute-start | bytes 3464 | tf_op jit(solution)/shard_map/ppermute | solution.py:18
  18.2 0.7 %copy-start.1 = (s32[11,16]{1,0:T(8,128)S(1)}, s32[11,16]{1,0:T(8,128)}, u32[]{:S(2)}) copy-start(s32[11,16]{1,0:T(8,128)} %param.14) | copy-start | bytes 2116
  18.2 0.7 %copy-start.3 = (f32[64]{0:T(128)S(1)}, f32[64]{0:T(128)}, u32[]{:S(2)}) copy-start(f32[64]{0:T(128)} %param.12) | copy-start | bytes 772
  19.5 0.7 %copy-start.4 = (f32[64]{0:T(128)S(1)}, f32[64]{0:T(128)}, u32[]{:S(2)}) copy-start(f32[64]{0:T(128)} %param.13) | copy-start | bytes 772
  19.6 0.7 %copy-start.5 = (s32[16]{0:T(128)S(1)}, s32[16]{0:T(128)}, u32[]{:S(2)}) copy-start(s32[16]{0:T(128)} %param.15) | copy-start | bytes 196
  21.4 0.7 %copy-start.2 = (f32[1,8,128]{2,1,0:T(8,128)S(1)}, f32[1,8,128]{2,1,0:T(8,128)}, u32[]{:S(2)}) copy-start(f32[1,8,128]{2,1,0:T(8,128)} %param.11) | copy-start | bytes 12292
  37.8 1.8 %collective-permute-start.3 = (f32[12,1,8,3]{3,2,1,0:T(8,128)S(1)}, f32[12,1,8,3]{3,2,1,0:T(8,128)S(1)}, u32[]{:S(2)}, u32[]{:S(2)}) collective-permute-start(f32[12,1,8,3]{3,2,1,0:T(8,128)S(1)} %get-tuple-element.32), channel_id=1, source_target_pairs={{1,0},{2,1},{3,2},{0,3},{5,4},{6,5},{7,6},{4,7},{9,8},{10,9},{11,1... | collective-permute-start | bytes 3464 | tf_op jit(solution)/shard_map/ppermute | solution.py:21
  37.9 3.6 %collective-permute-start.2 = (f32[12,1,8,3]{3,2,1,0:T(8,128)S(1)}, f32[12,1,8,3]{3,2,1,0:T(8,128)S(1)}, u32[]{:S(2)}, u32[]{:S(2)}) collective-permute-start(f32[12,1,8,3]{3,2,1,0:T(8,128)S(1)} %get-tuple-element.33), channel_id=1, source_target_pairs={{0,1},{1,2},{2,3},{3,0},{4,5},{5,6},{6,7},{7,4},{8,9},{9,10},{10,1... | collective-permute-start | bytes 3464 | tf_op jit(solution)/shard_map/ppermute | solution.py:18
where the time goes:
time: 42.6 us; the launch traced here: 42.3 us
  blocking collectives  27.9 us (65%)
  other arithmetic  4.04 us (9%)
  local copies, waits for them, and re-layouts  3.18 us (7%)
  starting transfers between devices  2.94 us (7%)
  waiting for transfers between devices  2.52 us (6%)
  between operations  0.89 us (2%)
  matrix products  0.84 us (2%)
    all_gather x2, blocking collectives, radiate(): gathered = lax.all_gather(line_data, 'wall', axis=1, tiled=True)  27.9 us
    ppermute x2, starting transfers between devices, with_halo(): lax.ppermute(lax.slice_in_dim(block, 0, width, axis=dim), axis, backward)  2.44 us
    unnamed x14, local copies, waits for them, and re-layouts  2 us
    ppermute x2, waiting for transfers between devices, with_halo(): lax.ppermute(lax.slice_in_dim(block, block.shape[dim] - width, None, axis...  1.79 us
    slice x2, local copies, waits for them, and re-layouts, with_halo(): lax.slice_in_dim(block, 0, width, axis=dim)  1.05 us
    another operation x6, other arithmetic, viewing_line_irradiance(): lax.cumsum(optical_thickness_step, viewing_line_dimension)  1.01 us
    another operation x4, other arithmetic, viewing_line_irradiance(): lax.cumsum(radiated_energy_rate * falloff, viewing_line_dimension, revers...  0.98 us
  transfers between devices with their start and end apart: 4, of which 2 were waited for; matrix products, arithmetic and copies ran while one was open for 6% of the time, Pallas kernels for 0%

commit v1 on v0

--- a/solution.py
+++ b/solution.py
@@ -107,7 +107,16 @@
     line_data = jnp.transpose(current, (0, 2, 1, 3)).reshape(
         components, row_count, stations * col_count
     )
-    gathered = lax.all_gather(line_data, "wall", axis=1, tiled=True)
+    ways = lax.axis_size("wall")
+    up = [(d, (d + 1) % ways) for d in range(ways)]
+    down = [(d, (d - 1) % ways) for d in range(ways)]
+    earlier, later = ([line_data], [line_data])
+    for _ in range(ways // 2):
+        earlier.append(lax.ppermute(earlier[-1], "wall", up))
+    for _ in range((ways - 1) // 2):
+        later.append(lax.ppermute(later[-1], "wall", down))
+    line = jnp.concatenate([*earlier[::-1], *later[1:]], axis=1)
+    gathered = jnp.roll(line, (lax.axis_index("wall") - ways // 2) * line_data.shape[1], axis=1)
     net_flux, wall_flux = viewing_line_irradiance(
         gathered[0],
         gathered[1:],

time: 42.6 us -> 35.7 us (0.84)
  blocking collectives: 27.9 us -> 0 us
  waiting for transfers between devices: 2.52 us -> 16.1 us
  starting transfers between devices: 2.94 us -> 10.1 us
  other arithmetic: 4.04 us -> 4.59 us
    all_gather x2 -> x0, blocking collectives: 27.9 us -> none  [radiate(): gathered = lax.all_gather(line_data, 'wall', axis=1, tiled=True)]
    ppermute x0 -> x6, waiting for transfers between devices: none -> 16.1 us  [the longest x4 15.8 us: radiate(): earlier.append(lax.ppermute(earlier[-1], 'wall', up))]
    ppermute x0 -> x6, starting transfers between devices: none -> 8.93 us  [the longest x2 8.92 us: radiate(): later.append(lax.ppermute(later[-1], 'wall', down))]
    ppermute x2, waiting for transfers between devices: 1.79 us -> 0.01 us  [with_halo(): lax.ppermute(lax.slice_in_dim(block, block.shape[dim] - width, None, axis...]
    ppermute x2, starting transfers between devices: 2.44 us -> 0.71 us  [with_halo(): lax.ppermute(lax.slice_in_dim(block, 0, width, axis=dim), axis, backward)]
    slice x2, local copies, waits for them, and re-layouts: 1.05 us -> 0.15 us  [with_halo(): lax.slice_in_dim(block, 0, width, axis=dim)]
    ppermute x2, waiting for transfers between devices: 0.73 us -> 0.01 us  [with_halo(): lax.ppermute(lax.slice_in_dim(block, 0, width, axis=dim), axis, backward)]
    unnamed x14, local copies, waits for them, and re-layouts: 2 us -> 2.69 us
  transfers between devices with their start and end apart: 4 -> 10, of which waited for: 2 -> 5; matrix products, arithmetic and copies ran while one was open for 6% -> 2% of each run, Pallas kernels for 0% -> 0%
where the time goes in v1:
time: 35.7 us; the launch traced here: 35.5 us
  waiting for transfers between devices  16.1 us (45%)
  starting transfers between devices  10.1 us (28%)
  other arithmetic  4.59 us (13%)
  local copies, waits for them, and re-layouts  2.87 us (8%)
  between operations  0.92 us (3%)
  matrix products  0.87 us (2%)
    ppermute x4, waiting for transfers between devices, radiate(): earlier.append(lax.ppermute(earlier[-1], 'wall', up))  15.8 us
    ppermute x2, starting transfers between devices, radiate(): later.append(lax.ppermute(later[-1], 'wall', down))  8.92 us
    unnamed x14, local copies, waits for them, and re-layouts  2.69 us
    another operation x6, other arithmetic, viewing_line_irradiance(): lax.cumsum(optical_thickness_step, viewing_line_dimension)  1.01 us
    another operation x4, other arithmetic, viewing_line_irradiance(): lax.cumsum(radiated_energy_rate * falloff, viewing_line_dimension, revers...  0.98 us
    dot_general x2, matrix products, viewing_line_irradiance(): jnp.einsum('kb,kij->bij', spectral_absorber_area, species_concentrations,...  0.87 us
    ppermute x2, starting transfers between devices, with_halo(): lax.ppermute(lax.slice_in_dim(block, 0, width, axis=dim), axis, backward)  0.71 us
  transfers between devices with their start and end apart: 10, of which 5 were waited for; matrix products, arithmetic and copies ran while one was open for 2% of the time, Pallas kernels for 0%

profile of v1, /device:TPU:0, one launch (start us, length us, event | category | flops | bytes accessed | tf_op | source)
XLA Modules:
  0.0 35.5 jit_solution(6811547295277389589)
XLA Ops:
  0.6 0.0 copy-start
  0.6 0.9 %copy.47 = f32[12,1,8,128]{3,0,2,1:T(8,128)S(1)} copy(f32[12,1,8,128]{3,2,1,0:T(8,128)} %param.12) | data formatting | bytes 98304 | tf_op args[0]
  1.5 5.1 %collective-permute-start.4 = (f32[12,8,128]{2,0,1:T(8,128)S(1)}, f32[12,8,128]{2,0,1:T(8,128)S(1)}, u32[]{:S(2)}, u32[]{:S(2)}) collective-permute-start(f32[12,8,128]{2,0,1:T(8,128)S(1)} %bitcast.36), channel_id=1, source_target_pairs={{0,12},{4,0},{8,4},{12,8},{1,13},{5,1},{9,5},{13,9},{2,14},{6,2},{... | collective-permute-start | bytes 147464 | tf_op jit(solution)/shard_map/ppermute | solution.py:117
  6.6 0.0 collective-permute-start.2
  6.6 0.0 copy-done
  6.6 0.1 fusion.86
  6.7 0.7 %collective-permute-start.1 = (f32[12,1,8,3]{3,2,1,0:T(8,128)S(1)}, f32[12,1,8,3]{3,2,1,0:T(8,128)S(1)}, u32[]{:S(2)}, u32[]{:S(2)}) collective-permute-start(f32[12,1,8,3]{3,2,1,0:T(8,128)S(1)} %get-tuple-element.33), channel_id=1, source_target_pairs={{1,0},{2,1},{3,2},{0,3},{5,4},{6,5},{7,6},{4,7},{9,8},{10,9},{11,1... | collective-permute-start | bytes 3464 | tf_op jit(solution)/shard_map/ppermute | solution.py:21
  7.4 0.0 collective-permute-start
  7.4 0.0 copy-start.1
  7.4 0.7 %copy-done.2 = f32[1,8,128]{2,1,0:T(8,128)S(1)} copy-done((f32[1,8,128]{2,1,0:T(8,128)S(1)}, f32[1,8,128]{2,1,0:T(8,128)}, u32[]{:S(2)}) %copy-start.2) | copy-done | bytes 4120
  8.1 0.6 %copy-done.4 = f32[64]{0:T(128)S(1)} copy-done((f32[64]{0:T(128)S(1)}, f32[64]{0:T(128)}, u32[]{:S(2)}) %copy-start.4) | copy-done | bytes 280
  8.7 0.0 copy-done.5
  8.7 0.2 select_reduce_fusion.1
  8.9 0.5 %copy-done.3 = f32[64]{0:T(128)S(1)} copy-done((f32[64]{0:T(128)S(1)}, f32[64]{0:T(128)}, u32[]{:S(2)}) %copy-start.3) | copy-done | bytes 280
  9.4 0.2 select_reduce_fusion
  9.6 0.0 collective-permute-done.1
  9.6 3.1 %collective-permute-done.2 = f32[12,8,128]{2,0,1:T(8,128)S(1)} collective-permute-done((f32[12,8,128]{2,0,1:T(8,128)S(1)}, f32[12,8,128]{2,0,1:T(8,128)S(1)}, u32[]{:S(2)}, u32[]{:S(2)}) %collective-permute-start.2) | collective-permute-done | bytes 49184 | tf_op jit(solution)/shard_map/ppermute | solution.py:115
  12.7 0.0 collective-permute-start.3
  12.7 0.0 collective-permute-done
  12.7 0.2 multiply_subtract_fusion.1
  12.9 0.0 collective-permute-done.4
  12.9 5.9 %collective-permute-done.3 = f32[12,8,128]{2,0,1:T(8,128)S(1)} collective-permute-done((f32[12,8,128]{2,0,1:T(8,128)S(1)}, f32[12,8,128]{2,0,1:T(8,128)S(1)}, u32[]{:S(2)}, u32[]{:S(2)}) %collective-permute-start.3) | collective-permute-done | bytes 49184 | tf_op jit(solution)/shard_map/ppermute | solution.py:115
  18.7 0.4 %fusion.7 = f32[12,32,128]{2,0,1:T(8,128)S(1)} fusion(s32[]{:T(128)S(6)} %select_n.28, f32[12,8,128]{2,0,1:T(8,128)S(1)} %collective-permute-done.3, f32[12,8,128]{2,0,1:T(8,128)S(1)} %collective-permute-done.2, f32[12,8,128]{2,0,1:T(8,128)S(1)} %bitcast.38, f32[12,8,128]{2,0,1:T(8,128)S(1)} %collective-permute-done.4), kind=kLoop, calls=%fused_computation.29 | loop fusion | flops 344064 | bytes 393220 | tf_op jit(solution)/shard_map/jit(_roll_dynamic)/concatenate | solution.py:119
  19.2 0.4 %fusion.11 = f32[16,32,128]{2,0,1:T(8,128)S(1)} fusion(f32[12,32,128]{2,0,1:T(8,128)S(1)} %fusion.7, f32[11,16]{1,0:T(8,128)S(1)} %select_reduce_fusion), kind=kOutput, calls=%fused_computation.33 | convolution fusion | flops 8650752 | bytes 459456 | tf_op jit(solution)/shard_map/kb,kij->bij/dot_general | solution.py:45
  19.7 0.2 fusion.25
  19.9 0.2 fusion.30
  20.2 0.2 fusion.89
  20.4 0.2 fusion.90
  20.8 0.1 fusion.85
  20.8 0.0 collective-permute-start.7
  20.9 0.1 collective-permute-start.6
  20.9 0.5 %collective-permute-start.5 = (f32[12,1,8,3]{3,2,1,0:T(8,128)S(1)}, f32[12,1,8,3]{3,2,1,0:T(8,128)S(1)}, u32[]{:S(2)}, u32[]{:S(2)}) collective-permute-start(f32[12,1,8,3]{3,2,1,0:T(8,128)S(1)} %get-tuple-element.32), channel_id=1, source_target_pairs={{0,1},{1,2},{2,3},{3,0},{4,5},{5,6},{6,7},{7,4},{8,9},{9,10},{10,1... | collective-permute-start | bytes 3464 | tf_op jit(solution)/shard_map/ppermute | solution.py:18
  21.4 3.8 %collective-permute-start.9 = (f32[12,8,128]{2,1,0:T(8,128)S(1)}, f32[12,8,128]{2,1,0:T(8,128)S(1)}, u32[]{:S(2)}, u32[]{:S(2)}) collective-permute-start(f32[12,8,128]{2,1,0:T(8,128)S(1)} %bitcast.30), channel_id=1, source_target_pairs={{0,12},{4,0},{8,4},{12,8},{1,13},{5,1},{9,5},{13,9},{2,14},{6,2},{... | collective-permute-start | bytes 147464 | tf_op jit(solution)/shard_map/ppermute | solution.py:117
  25.2 1.5 %collective-permute-done.7 = f32[12,8,128]{2,1,0:T(8,128)S(1)} collective-permute-done((f32[12,8,128]{2,1,0:T(8,128)S(1)}, f32[12,8,128]{2,1,0:T(8,128)S(1)}, u32[]{:S(2)}, u32[]{:S(2)}) %collective-permute-start.7) | collective-permute-done | bytes 49184 | tf_op jit(solution)/shard_map/ppermute | solution.py:115
  26.7 0.0 collective-permute-start.8
  26.7 0.0 collective-permute-done.6
  26.7 0.0 collective-permute-done.5
  26.7 0.2 multiply_subtract_fusion
  27.0 0.3 collective-permute-done.9
  27.3 5.4 %collective-permute-done.8 = f32[12,8,128]{2,1,0:T(8,128)S(1)} collective-permute-done((f32[12,8,128]{2,1,0:T(8,128)S(1)}, f32[12,8,128]{2,1,0:T(8,128)S(1)}, u32[]{:S(2)}, u32[]{:S(2)}) %collective-permute-start.8) | collective-permute-done | bytes 49184 | tf_op jit(solution)/shard_map/ppermute | solution.py:115
  32.6 0.1 fusion.40
  32.8 0.5 %fusion.13 = f32[16,32,128]{2,0,1:T(8,128)S(1)} fusion(f32[11,32,128]{2,1,0:T(8,128)S(1)} %slice.233, f32[11,16]{1,0:T(8,128)S(1)} %select_reduce_fusion), kind=kOutput, calls=%fused_computation.35 | convolution fusion | flops 8650752 | bytes 443072 | tf_op jit(solution)/shard_map/kb,kij->bij/dot_general | solution.py:45
  33.3 0.2 fusion.15
  33.5 0.2 fusion.20
  33.8 0.2 fusion.91
  34.0 0.2 fusion.92
  34.3 0.6 %add_multiply_fusion = f32[12,1,8,128]{3,2,1,0:T(8,128)} fusion(f32[12,1,8,128]{3,2,1,0:T(8,128)S(1)} %constant_dynamic-update-slice_fusion.2, f32[12,1,8,128]{3,2,1,0:T(8,128)S(1)} %copy-done, f32[12,1,8,128]{3,2,1,0:T(8,128)S(1)} %add.114), kind=kLoop, calls=%fused_computation.106 | loop fusion | flops 36864 | bytes 196608 | tf_op jit(solution)/shard_map/mul | solution.py:158
  35.0 0.5 %multiply_bitcast_fusion.1 = f32[1,128]{1,0:T(1,128)} fusion(f32[128]{0:T(128)S(1)} %get-tuple-element.39, f32[128]{0:T(128)S(1)} %get-tuple-element.40, f32[128]{0:T(128)S(1)} %get-tuple-element.41, f32[128]{0:T(128)S(1)} %get-tuple-element.42), kind=kLoop, calls=%fused_computation.147 | loop fusion | flops 1024 | bytes 2560 | tf_op jit(solution)/shard_map/mul | solution.py:159
  (24 shorter events, 0.3 us)
Async XLA Ops:
  0.6 6.0 %copy-start = (f32[12,1,8,128]{3,2,1,0:T(8,128)S(1)}, f32[12,1,8,128]{3,2,1,0:T(8,128)}, u32[]{:S(2)}) copy-start(f32[12,1,8,128]{3,2,1,0:T(8,128)} %param.12) | copy-start | bytes 147460
  1.5 11.4 %collective-permute-start.4 = (f32[12,8,128]{2,0,1:T(8,128)S(1)}, f32[12,8,128]{2,0,1:T(8,128)S(1)}, u32[]{:S(2)}, u32[]{:S(2)}) collective-permute-start(f32[12,8,128]{2,0,1:T(8,128)S(1)} %bitcast.36), channel_id=1, source_target_pairs={{0,12},{4,0},{8,4},{12,8},{1,13},{5,1},{9,5},{13,9},{2,14},{6,2},{... | collective-permute-start | bytes 147464 | tf_op jit(solution)/shard_map/ppermute | solution.py:117
  6.6 6.1 %collective-permute-start.2 = (f32[12,8,128]{2,0,1:T(8,128)S(1)}, f32[12,8,128]{2,0,1:T(8,128)S(1)}, u32[]{:S(2)}, u32[]{:S(2)}) collective-permute-start(f32[12,8,128]{2,0,1:T(8,128)S(1)} %bitcast.37), channel_id=1, source_target_pairs={{0,4},{4,8},{8,12},{12,0},{1,5},{5,9},{9,13},{13,1},{2,6},{6,10},{... | collective-permute-start | bytes 147464 | tf_op jit(solution)/shard_map/ppermute | solution.py:115
  6.7 2.9 %collective-permute-start.1 = (f32[12,1,8,3]{3,2,1,0:T(8,128)S(1)}, f32[12,1,8,3]{3,2,1,0:T(8,128)S(1)}, u32[]{:S(2)}, u32[]{:S(2)}) collective-permute-start(f32[12,1,8,3]{3,2,1,0:T(8,128)S(1)} %get-tuple-element.33), channel_id=1, source_target_pairs={{1,0},{2,1},{3,2},{0,3},{5,4},{6,5},{7,6},{4,7},{9,8},{10,9},{11,1... | collective-permute-start | bytes 3464 | tf_op jit(solution)/shard_map/ppermute | solution.py:21
  7.4 5.3 %collective-permute-start = (f32[12,1,8,3]{3,2,1,0:T(8,128)S(1)}, f32[12,1,8,3]{3,2,1,0:T(8,128)S(1)}, u32[]{:S(2)}, u32[]{:S(2)}) collective-permute-start(f32[12,1,8,3]{3,2,1,0:T(8,128)S(1)} %get-tuple-element.34), channel_id=1, source_target_pairs={{0,1},{1,2},{2,3},{3,0},{4,5},{5,6},{6,7},{7,4},{8,9},{9,10},{10,1... | collective-permute-start | bytes 3464 | tf_op jit(solution)/shard_map/ppermute | solution.py:18
  7.4 0.7 %copy-start.2 = (f32[1,8,128]{2,1,0:T(8,128)S(1)}, f32[1,8,128]{2,1,0:T(8,128)}, u32[]{:S(2)}) copy-start(f32[1,8,128]{2,1,0:T(8,128)} %param.13) | copy-start | bytes 12292
  7.4 1.5 %copy-start.1 = (s32[11,16]{1,0:T(8,128)S(1)}, s32[11,16]{1,0:T(8,128)}, u32[]{:S(2)}) copy-start(s32[11,16]{1,0:T(8,128)} %param.16) | copy-start | bytes 2116
  8.1 0.7 %copy-start.4 = (f32[64]{0:T(128)S(1)}, f32[64]{0:T(128)}, u32[]{:S(2)}) copy-start(f32[64]{0:T(128)} %param.15) | copy-start | bytes 772
  8.1 0.7 %copy-start.5 = (s32[16]{0:T(128)S(1)}, s32[16]{0:T(128)}, u32[]{:S(2)}) copy-start(s32[16]{0:T(128)} %param.17) | copy-start | bytes 196
  8.7 0.7 %copy-start.3 = (f32[64]{0:T(128)S(1)}, f32[64]{0:T(128)}, u32[]{:S(2)}) copy-start(f32[64]{0:T(128)} %param.14) | copy-start | bytes 772
  12.7 6.1 %collective-permute-start.3 = (f32[12,8,128]{2,0,1:T(8,128)S(1)}, f32[12,8,128]{2,0,1:T(8,128)S(1)}, u32[]{:S(2)}, u32[]{:S(2)}) collective-permute-start(f32[12,8,128]{2,0,1:T(8,128)S(1)} %collective-permute-done.2), channel_id=1, source_target_pairs={{0,4},{4,8},{8,12},{12,0},{1,5},{5,9},{9,13},{13,1},{2,6},{6,10},{... | collective-permute-start | bytes 147464 | tf_op jit(solution)/shard_map/ppermute | solution.py:115
  20.8 5.9 %collective-permute-start.7 = (f32[12,8,128]{2,1,0:T(8,128)S(1)}, f32[12,8,128]{2,1,0:T(8,128)S(1)}, u32[]{:S(2)}, u32[]{:S(2)}) collective-permute-start(f32[12,8,128]{2,1,0:T(8,128)S(1)} %bitcast.29), channel_id=1, source_target_pairs={{0,4},{4,8},{8,12},{12,0},{1,5},{5,9},{9,13},{13,1},{2,6},{6,10},{... | collective-permute-start | bytes 147464 | tf_op jit(solution)/shard_map/ppermute | solution.py:115
  20.9 5.9 %collective-permute-start.6 = (f32[12,1,8,3]{3,2,1,0:T(8,128)S(1)}, f32[12,1,8,3]{3,2,1,0:T(8,128)S(1)}, u32[]{:S(2)}, u32[]{:S(2)}) collective-permute-start(f32[12,1,8,3]{3,2,1,0:T(8,128)S(1)} %get-tuple-element.31), channel_id=1, source_target_pairs={{1,0},{2,1},{3,2},{0,3},{5,4},{6,5},{7,6},{4,7},{9,8},{10,9},{11,1... | collective-permute-start | bytes 3464 | tf_op jit(solution)/shard_map/ppermute | solution.py:21
  20.9 5.8 %collective-permute-start.5 = (f32[12,1,8,3]{3,2,1,0:T(8,128)S(1)}, f32[12,1,8,3]{3,2,1,0:T(8,128)S(1)}, u32[]{:S(2)}, u32[]{:S(2)}) collective-permute-start(f32[12,1,8,3]{3,2,1,0:T(8,128)S(1)} %get-tuple-element.32), channel_id=1, source_target_pairs={{0,1},{1,2},{2,3},{3,0},{4,5},{5,6},{6,7},{7,4},{8,9},{9,10},{10,1... | collective-permute-start | bytes 3464 | tf_op jit(solution)/shard_map/ppermute | solution.py:18
  21.4 5.8 %collective-permute-start.9 = (f32[12,8,128]{2,1,0:T(8,128)S(1)}, f32[12,8,128]{2,1,0:T(8,128)S(1)}, u32[]{:S(2)}, u32[]{:S(2)}) collective-permute-start(f32[12,8,128]{2,1,0:T(8,128)S(1)} %bitcast.30), channel_id=1, source_target_pairs={{0,12},{4,0},{8,4},{12,8},{1,13},{5,1},{9,5},{13,9},{2,14},{6,2},{... | collective-permute-start | bytes 147464 | tf_op jit(solution)/shard_map/ppermute | solution.py:117
  26.7 5.9 %collective-permute-start.8 = (f32[12,8,128]{2,1,0:T(8,128)S(1)}, f32[12,8,128]{2,1,0:T(8,128)S(1)}, u32[]{:S(2)}, u32[]{:S(2)}) collective-permute-start(f32[12,8,128]{2,1,0:T(8,128)S(1)} %collective-permute-done.7), channel_id=1, source_target_pairs={{0,4},{4,8},{8,12},{12,0},{1,5},{5,9},{9,13},{13,1},{2,6},{6,10},{... | collective-permute-start | bytes 147464 | tf_op jit(solution)/shard_map/ppermute | solution.py:115
